TPU v7x, 512 devices: a whole 4x8x8 slice. The times are simulated.
512 devices in a mesh: dp: 64 (over x, y_lo, z), ctx: 8 (over y_hi, core).
Axes of the slice: x: 4, y: 8 (y_hi: 4, y_lo: 2; y = y_hi * 2 + y_lo), z: 8, core: 2. Of those that a mesh axis runs over, the one named last changes fastest.
Arguments:
- query_in: bfloat16 [64, 1024, 1024], P('dp', 'ctx'), may hold values from -6 to 6
- key_in: bfloat16 [64, 1024, 1024], P('dp', 'ctx'), may hold values from -6 to 6
- value_in: bfloat16 [64, 1024, 1024], P('dp', 'ctx'), may hold values from -6 to 6
- gate_in: bfloat16 [64, 1024, 1024], P('dp', 'ctx'), may hold values from -6 to 6
- out_grad: bfloat16 [64, 1024, 1024], P('dp', 'ctx'), may hold values from -6 to 6
- out_weight: bfloat16 [1024, 1024], P('dp'), may hold values from -0.1875 to 0.1875
- lengths: int32 [64, 8], P('dp'), may hold values from 1 to 512, 1024 in all within a row
- stamps: int32 [64, 1024], P('dp'), may hold values from 1 to 6291456, as said below
- pos_bias: float32 [1024], replicated, may hold values from -3 to 3
- time_bias: float32 [32], replicated, may hold values from -3 to 3
Outputs:
- layer_out: bfloat16 [64, 1024, 1024], P('dp', 'ctx')
- query_grad: bfloat16 [64, 1024, 1024], P('dp', 'ctx')
- key_grad: bfloat16 [64, 1024, 1024], P('dp', 'ctx')
- value_grad: bfloat16 [64, 1024, 1024], P('dp', 'ctx')
- gate_grad: bfloat16 [64, 1024, 1024], P('dp', 'ctx')
- weight_grad: float32 [1024, 1024], P('dp')
- pos_grad: float32 [1024], replicated
- time_grad: float32 [32], replicated
Inputs may be any that keep to these rules, and one draw needn't show every extreme that they name: In every pack the 8 lengths add up to 1024 and the longest is exactly 512. `stamps`: timestamps rise strictly along each pack; each pack's first is 1 and its last is 6291456.
All inputs are finite; a program needn't handle non-finite values.
Results may differ from a plain program's by a relative error of at most 0.015.
Values may be sent and summed in bfloat16 or wider, within the bound.
A program may use at most 64 MiB of HBM per device.

v0:
```python
import jax
import jax.numpy as jnp
from jax import lax
from jax.sharding import PartitionSpec as P

HEAD_DIM = 128
EPSILON = 1e-06


def bucket_of(time_gap):
    bucket = jnp.zeros(time_gap.shape, jnp.int32)
    for shift_by in range(31):
        bucket = bucket + (time_gap >= 1 << shift_by).astype(jnp.int32)
    return bucket


def toeplitz(table, offset, row_total, col_total):
    length = table.shape[0]
    extended = jnp.concatenate(
        [jnp.zeros((length + col_total,), table.dtype), table, jnp.zeros((row_total,), table.dtype)]
    )
    diag_span = row_total + col_total - 1
    window = lax.dynamic_slice_in_dim(extended, length + offset + 1, diag_span)
    flipped = window[::-1]
    repeated = jnp.tile(flipped, row_total + 1)[: row_total * (diag_span + 1)]
    sliding = repeated.reshape(row_total, diag_span + 1)[:, :col_total]
    return sliding[::-1]


def block_bias(pos_table, time_table, query_stamps, key_stamps, offset):
    row_total = query_stamps.shape[0]
    col_total = key_stamps.shape[0]
    bucket = bucket_of(jnp.abs(query_stamps[:, None] - key_stamps[None, :]))
    timed = jnp.zeros((row_total, col_total), jnp.float32)
    for bucket_no in range(time_table.shape[0]):
        timed = timed + jnp.where(bucket == bucket_no, time_table[bucket_no], 0.0)
    return toeplitz(pos_table, offset, row_total, col_total) + timed


def split_heads(block_rows):
    return block_rows.reshape(block_rows.shape[0], block_rows.shape[1] // HEAD_DIM, HEAD_DIM)


def score_grads(scores, pair_mask, grad_block, value_block):
    weight_grads = jnp.einsum(
        "rhd,chd->hrc",
        split_heads(grad_block),
        split_heads(value_block),
        preferred_element_type=jnp.float32,
    )
    gate_sig = jax.nn.sigmoid(scores)
    return jnp.where(
        pair_mask[None], weight_grads * gate_sig * (1.0 + scores * (1.0 - gate_sig)), 0.0
    )


def on_device(
    query_in, key_in, value_in, gate_in, out_grad, out_weight, lengths, stamps, pos_bias, time_bias
):
    query_mine = query_in[0]
    key_mine = key_in[0]
    value_mine = value_in[0]
    gate_mine = gate_in[0]
    grad_mine = out_grad[0]
    row_count = query_mine.shape[0]
    context = stamps.shape[1]
    stamp_row = stamps[0]
    user_ends = jnp.cumsum(lengths[0])
    places = lax.iota(jnp.int32, context)
    user_ids = jnp.sum((places[:, None] >= user_ends[None, :]).astype(jnp.int32), axis=1)
    my_first = lax.axis_index("ctx") * row_count
    factor = HEAD_DIM ** (-0.5)

    def pair_terms(query_block, key_block, query_first, key_first):
        query_size = query_block.shape[0]
        key_size = key_block.shape[0]
        query_users = lax.dynamic_slice_in_dim(user_ids, query_first, query_size)
        key_users = lax.dynamic_slice_in_dim(user_ids, key_first, key_size)
        query_stamps = lax.dynamic_slice_in_dim(stamp_row, query_first, query_size)
        key_stamps = lax.dynamic_slice_in_dim(stamp_row, key_first, key_size)
        query_places = query_first + lax.iota(jnp.int32, query_size)
        key_places = key_first + lax.iota(jnp.int32, key_size)
        pair_mask = (query_users[:, None] == key_users[None, :]) & (
            query_places[:, None] >= key_places[None, :]
        )

        def bias_of(table_pos, table_time):
            return block_bias(
                table_pos, table_time, query_stamps, key_stamps, query_first - key_first
            )

        pair_bias, pull_back = jax.vjp(bias_of, pos_bias, time_bias)
        scores = (
            jnp.einsum(
                "rhd,chd->hrc",
                split_heads(query_block),
                split_heads(key_block),
                preferred_element_type=jnp.float32,
            )
            * factor
            + pair_bias[None]
        )
        return (scores, pair_mask, pull_back)

    key_all, value_all = (
        lax.all_gather(key_mine, "ctx", axis=0, tiled=True),
        lax.all_gather(value_mine, "ctx", axis=0, tiled=True),
    )
    query_size = min(512, query_mine.shape[0])
    key_size = min(512, key_all.shape[0])
    col_count = query_mine.shape[1]

    def forward_per_query(query_step):
        query_start = my_first + query_step * query_size

        def forward_per_key(carried, key_step):
            key_start = 0 + key_step * key_size
            key_block = lax.dynamic_slice_in_dim(key_all, key_step * key_size, key_size)
            value_block = lax.dynamic_slice_in_dim(value_all, key_step * key_size, key_size)
            scores, pair_mask, pull_back = pair_terms(query_mine, key_block, query_start, key_start)
            weights = jnp.where(pair_mask[None], jax.nn.silu(scores), 0.0).astype(jnp.bfloat16)
            attended_part = jnp.einsum(
                "hrc,chd->rhd",
                weights,
                split_heads(value_block),
                preferred_element_type=jnp.float32,
            )
            return (carried + attended_part.reshape(query_size, col_count), None)

        zeros_init = jnp.zeros((query_size, col_count), jnp.float32)
        result, unused = lax.scan(
            forward_per_key, zeros_init, lax.iota(jnp.int32, key_all.shape[0] // key_size)
        )
        return result

    outputs = lax.map(forward_per_query, lax.iota(jnp.int32, query_mine.shape[0] // query_size))
    attended = outputs.reshape(query_mine.shape).astype(jnp.bfloat16)
    attended_wide = attended.astype(jnp.float32)
    center = attended_wide - jnp.mean(attended_wide, axis=1, keepdims=True)
    inv_dev = lax.rsqrt(jnp.mean(center * center, axis=1, keepdims=True) + EPSILON)
    normed = center * inv_dev
    gate_wide = gate_mine.astype(jnp.float32)
    mixed_rows = (normed * gate_wide).astype(jnp.bfloat16)
    contract_cols = (((1,), (1,)), ((), ()))
    whole_rows = lax.all_gather(out_weight, "dp", axis=0, tiled=True)
    layer_out = jnp.dot(mixed_rows, whole_rows, preferred_element_type=jnp.float32)
    mixed_grad = lax.dot_general(
        grad_mine, whole_rows, contract_cols, preferred_element_type=jnp.float32
    )
    weight_part = lax.psum_scatter(
        lax.dot_general(
            mixed_rows, grad_mine, (((0,), (0,)), ((), ())), preferred_element_type=jnp.float32
        ),
        "dp",
        scatter_dimension=0,
        tiled=True,
    )
    weight_grad = lax.psum(weight_part, "ctx")
    gate_grad = (mixed_grad * normed).astype(jnp.bfloat16)
    normed_grad = mixed_grad * gate_wide
    attn_grad = inv_dev * (
        normed_grad
        - jnp.mean(normed_grad, axis=1, keepdims=True)
        - normed * jnp.mean(normed_grad * normed, axis=1, keepdims=True)
    )
    attn_grad = attn_grad.astype(jnp.bfloat16)
    grad_rows = attn_grad
    query_query_size = min(512, query_mine.shape[0])
    query_key_size = min(512, key_all.shape[0])
    query_col_count = query_mine.shape[1]

    def query_per_query(query_step):
        query_start = my_first + query_step * query_query_size

        def query_per_key(carried, key_step):
            key_start = 0 + key_step * query_key_size
            key_block = lax.dynamic_slice_in_dim(key_all, key_step * query_key_size, query_key_size)
            value_block = lax.dynamic_slice_in_dim(
                value_all, key_step * query_key_size, query_key_size
            )
            scores, pair_mask, pull_back = pair_terms(query_mine, key_block, query_start, key_start)
            score_grad = score_grads(scores, pair_mask, grad_rows, value_block)
            pos_part, time_part = pull_back(jnp.sum(score_grad, axis=0))
            query_part = jnp.einsum(
                "hrc,chd->rhd",
                score_grad.astype(jnp.bfloat16),
                split_heads(key_block),
                preferred_element_type=jnp.float32,
            )
            return (
                (
                    carried[0] + query_part.reshape(query_query_size, query_col_count),
                    carried[1] + pos_part,
                    carried[2] + time_part,
                ),
                None,
            )

        zeros_init = (
            jnp.zeros((query_query_size, query_col_count), jnp.float32),
            jnp.zeros(pos_bias.shape, jnp.float32),
            jnp.zeros(time_bias.shape, jnp.float32),
        )
        result, unused = lax.scan(
            query_per_key, zeros_init, lax.iota(jnp.int32, key_all.shape[0] // query_key_size)
        )
        return result

    query_sums, pos_sums, time_sums = lax.map(
        query_per_query, lax.iota(jnp.int32, query_mine.shape[0] // query_query_size)
    )
    query_grad = (query_sums.reshape(query_mine.shape) * factor).astype(jnp.bfloat16)
    query_grad, pos_local, time_local = (
        query_grad,
        jnp.sum(pos_sums, axis=0),
        jnp.sum(time_sums, axis=0),
    )
    query_all, grad_all = (
        lax.all_gather(query_mine, "ctx", axis=0, tiled=True),
        lax.all_gather(attn_grad, "ctx", axis=0, tiled=True),
    )
    key_query_size = min(512, query_all.shape[0])
    key_key_size = min(512, key_mine.shape[0])
    key_col_count = key_mine.shape[1]

    def key_per_key(key_step):
        key_start = my_first + key_step * key_key_size

        def per_per_query(carried, query_step):
            query_start = 0 + query_step * key_query_size
            query_block = lax.dynamic_slice_in_dim(
                query_all, query_step * key_query_size, key_query_size
            )
            grad_block = lax.dynamic_slice_in_dim(
                grad_all, query_step * key_query_size, key_query_size
            )
            scores, pair_mask, pull_back = pair_terms(query_block, key_mine, query_start, key_start)
            weights = jnp.where(pair_mask[None], jax.nn.silu(scores), 0.0).astype(jnp.bfloat16)
            score_grad = score_grads(scores, pair_mask, grad_block, value_mine)
            value_part = jnp.einsum(
                "hrc,rhd->chd", weights, split_heads(grad_block), preferred_element_type=jnp.float32
            )
            key_part = jnp.einsum(
                "hrc,rhd->chd",
                score_grad.astype(jnp.bfloat16),
                split_heads(query_block),
                preferred_element_type=jnp.float32,
            )
            return (
                (
                    carried[0] + key_part.reshape(key_key_size, key_col_count),
                    carried[1] + value_part.reshape(key_key_size, key_col_count),
                ),
                None,
            )

        zero_rows = jnp.zeros((key_key_size, key_col_count), jnp.float32)
        result, unused = lax.scan(
            per_per_query,
            (zero_rows, zero_rows),
            lax.iota(jnp.int32, query_all.shape[0] // key_query_size),
        )
        return result

    key_sums, value_sums = lax.map(
        key_per_key, lax.iota(jnp.int32, key_mine.shape[0] // key_key_size)
    )
    key_grad = (key_sums.reshape(key_mine.shape) * factor).astype(jnp.bfloat16)
    key_grad, value_grad = (key_grad, value_sums.reshape(key_mine.shape).astype(jnp.bfloat16))
    pos_grad, time_grad = lax.psum((pos_local, time_local), ("dp", "ctx"))
    return (
        layer_out.astype(jnp.bfloat16)[None],
        query_grad[None],
        key_grad[None],
        value_grad[None],
        gate_grad[None],
        weight_grad,
        pos_grad,
        time_grad,
    )


def solution(mesh):
    placed = (
        P("dp", "ctx", None),
        P("dp", "ctx", None),
        P("dp", "ctx", None),
        P("dp", "ctx", None),
        P("dp", "ctx", None),
        P("dp", None),
        P("dp", None),
        P("dp", None),
        P(),
        P(),
    )
    return jax.shard_map(
        on_device,
        mesh=mesh,
        in_specs=placed,
        out_specs=(
            P("dp", "ctx", None),
            P("dp", "ctx", None),
            P("dp", "ctx", None),
            P("dp", "ctx", None),
            P("dp", "ctx", None),
            P("dp", None),
            P(),
            P(),
        ),
        check_vma=False,
    )
```

profile of v0, /device:TPU:17, one launch (start us, length us, event | category | flops | bytes accessed | tf_op | source)
XLA Modules:
  0.0 894.1 jit_solution(12226835931457690420)
XLA Ops:
  14.1 43.6 %all-gather.13.cloned.1.call-done = bf16[1,1024,1024]{1,2,0:T(8,128)(2,1)} async-done(((bf16[1,128,1024]{1,2,0:T(8,128)(2,1)}), bf16[1,1024,1024]{1,2,0:T(8,128)(2,1)}) %all-gather.13.cloned.1.call-update) | async-done | bytes 2097168 | tf_op jit(solution)/shard_map/all_gather | solution.py:107
  57.7 44.1 %all-gather.15.cloned.1.call-done = bf16[1,1024,1024]{1,2,0:T(8,128)(2,1)} async-done(((bf16[1,128,1024]{1,2,0:T(8,128)(2,1)}), bf16[1,1024,1024]{1,2,0:T(8,128)(2,1)}) %all-gather.15.cloned.1.call-update) | async-done | bytes 2097168 | tf_op jit(solution)/shard_map/all_gather | solution.py:106
  101.8 72.8 %while.78 = (s32[]{:T(128)}, f32[128,1024]{0,1:T(8,128)}, s32[2]{0:T(128)S(1)}, bf16[1024,1024]{0,1:T(8,128)(2,1)}, s32[128]{0:T(128)S(1)}, /*index=5*/s32[1024]...) while((s32[]{:T(128)}, f32[128,1024]{0,1:T(8,128)}, ...), condition=%wide.region_3.4_spmd.clone, body=%wide.region_2.3_spmd.clone.sunk | while | flops 285542272 | bytes 18211576 | solution.py:131
  109.5 21.8 %add_add_fusion.6 = f32[128,512]{1,0:T(8,128)S(1)} fusion(f32[128,512]{1,0:T(8,128)S(1)} %rev.84, f32[]{:T(128)} %bitcast.417, f32[]{:T(128)} %bitcast.418, f32[]{:T(128)} %bitcast.419, f32[]{:T(128)} %bitcast.420, f32[]{:T(128)} %bitcast.421, f32[]{:T(128)} %bitcast.422, f32[]{:T(128)} %bitcast.423, f32[]{:T(128)} %bitcast.424, f32[]{:T(128)} %bitcast.425, ...), kind=kLoop, calls=%fused_computation.10.clone.1 | loop fusion | flops 12451840 | bytes 526976 | tf_op jit(solution)/shard_map/while/body/eval_jaxpr/while/body/eval_jaxpr/jvp()/add | solution.py:37
  133.2 3.1 fusion.217
  145.9 21.8 %add_add_fusion.6 = f32[128,512]{1,0:T(8,128)S(1)} fusion(f32[128,512]{1,0:T(8,128)S(1)} %rev.84, f32[]{:T(128)} %bitcast.417, f32[]{:T(128)} %bitcast.418, f32[]{:T(128)} %bitcast.419, f32[]{:T(128)} %bitcast.420, f32[]{:T(128)} %bitcast.421, f32[]{:T(128)} %bitcast.422, f32[]{:T(128)} %bitcast.423, f32[]{:T(128)} %bitcast.424, f32[]{:T(128)} %bitcast.425, ...), kind=kLoop, calls=%fused_computation.10.clone.1 | loop fusion | flops 12451840 | bytes 526976 | tf_op jit(solution)/shard_map/while/body/eval_jaxpr/while/body/eval_jaxpr/jvp()/add | solution.py:37
  169.6 3.1 fusion.217
  176.2 185.8 %all-gather.9.cloned.1.call-done = bf16[1024,1024]{1,0:T(8,128)(2,1)} async-done(((bf16[16,1024]{1,0:T(8,128)(2,1)}), bf16[1024,1024]{1,0:T(8,128)(2,1)}) %all-gather.9.cloned.1.call-update) | async-done | bytes 2097168 | tf_op jit(solution)/shard_map/all_gather | solution.py:145
  362.0 2.5 fusion.156
  365.8 2.8 fusion.152
  370.1 150.5 %while.79 = (s32[]{:T(128)}, f32[128,1024]{0,1:T(8,128)}, f32[1024]{0:T(1024)S(1)}, f32[32]{0:T(128)S(1)}, s32[2]{0:T(128)S(1)}, /*index=5*/bf16[1024,1024]{0,1:...) while((s32[]{:T(128)}, f32[128,1024]{0,1:T(8,128)}, ...), condition=%wide.region_43.44_spmd.clone, body=%wide.region_8.43_spmd.clone.sunk | while | flops 434852608 | bytes 32417576 | solution.py:204
  383.9 3.1 rev.85
  388.5 22.5 %add_add_fusion.7 = f32[128,512]{0,1:T(8,128)S(1)} fusion(f32[128,512]{0,1:T(8,128)} %rev.85, f32[]{:T(128)} %bitcast.461, f32[]{:T(128)} %bitcast.462, f32[]{:T(128)} %bitcast.463, f32[]{:T(128)} %bitcast.464, f32[]{:T(128)} %bitcast.465, f32[]{:T(128)} %bitcast.466, f32[]{:T(128)} %bitcast.467, f32[]{:T(128)} %bitcast.468, f32[]{:T(128)} %bitcast.469, ...), kind=kLoop, calls=%fused_computation.100.clone.1 | loop fusion | flops 12451840 | bytes 526976 | tf_op jit(solution)/shard_map/while/body/eval_jaxpr/while/body/eval_jaxpr/jvp()/add | solution.py:37
  422.7 2.5 select_reduce_fusion.33
  425.2 20.1 %fusion.230 = f32[32]{0:T(128)S(1)} fusion(f32[32]{0:T(128)S(1)} %get-tuple-element.2032, pred[]{:T(512)S(6)} %compare.44, f32[1]{0:T(128)} %bitcast.497, f32[1]{0:T(128)} %bitcast.498, f32[1]{0:T(128)} %bitcast.499, f32[1]{0:T(128)} %bitcast.500, f32[1]{0:T(128)} %bitcast.501, f32[1]{0:T(128)} %bitcast.502, f32[1]{0:T(128)} %bitcast.503, ...), kind=kLoop, calls=%fused_computation.175.clone.1 | loop fusion | flops 1056 | bytes 385 | tf_op jit(solution)/shard_map/while/body/eval_jaxpr/while/body/eval_jaxpr/add | solution.py:194
  446.6 2.5 constant_dynamic-slice_fusion.11
  459.1 3.1 rev.85
  463.7 22.5 %add_add_fusion.7 = f32[128,512]{0,1:T(8,128)S(1)} fusion(f32[128,512]{0,1:T(8,128)} %rev.85, f32[]{:T(128)} %bitcast.461, f32[]{:T(128)} %bitcast.462, f32[]{:T(128)} %bitcast.463, f32[]{:T(128)} %bitcast.464, f32[]{:T(128)} %bitcast.465, f32[]{:T(128)} %bitcast.466, f32[]{:T(128)} %bitcast.467, f32[]{:T(128)} %bitcast.468, f32[]{:T(128)} %bitcast.469, ...), kind=kLoop, calls=%fused_computation.100.clone.1 | loop fusion | flops 12451840 | bytes 526976 | tf_op jit(solution)/shard_map/while/body/eval_jaxpr/while/body/eval_jaxpr/jvp()/add | solution.py:37
  498.1 2.5 select_reduce_fusion.33
  500.6 20.1 %fusion.230 = f32[32]{0:T(128)S(1)} fusion(f32[32]{0:T(128)S(1)} %get-tuple-element.2032, pred[]{:T(512)S(6)} %compare.44, f32[1]{0:T(128)} %bitcast.497, f32[1]{0:T(128)} %bitcast.498, f32[1]{0:T(128)} %bitcast.499, f32[1]{0:T(128)} %bitcast.500, f32[1]{0:T(128)} %bitcast.501, f32[1]{0:T(128)} %bitcast.502, f32[1]{0:T(128)} %bitcast.503, ...), kind=kLoop, calls=%fused_computation.175.clone.1 | loop fusion | flops 1056 | bytes 385 | tf_op jit(solution)/shard_map/while/body/eval_jaxpr/while/body/eval_jaxpr/add | solution.py:194
  521.9 141.3 %all-reduce.34 = (f32[1024]{0:T(1024)}, f32[32]{0:T(128)}) all-reduce(f32[1024]{0:T(1024)S(1)} %get-tuple-element.956, f32[32]{0:T(128)S(1)} %get-tuple-element.957), channel_id=1, replica_groups=mesh['dp'=64,'ctx'=8] {'dp','ctx'}, use_global_device_ids=true, to_apply=%region_48.49 | all-reduce | flops 1056 | bytes 8448 | tf_op jit(solution)/shard_map/psum | solution.py:270
  663.2 3.0 fusion.136
  666.9 88.4 %while.80 = (s32[]{:T(128)}, f32[128,1024]{0,1:T(8,128)}, f32[128,1024]{0,1:T(8,128)}, s32[2]{0:T(128)S(1)}, bf16[1024,1024]{0,1:T(8,128)(2,1)}, /*index=5*/s32[...) while((s32[]{:T(128)}, f32[128,1024]{0,1:T(8,128)}, ...), condition=%wide.region_45.46_spmd.clone, body=%wide.region_44.45_spmd.clone.sunk | while | flops 560531328 | bytes 61329784 | solution.py:258
  677.5 21.7 %add_add_fusion.8 = f32[512,128]{1,0:T(8,128)S(1)} fusion(f32[512,128]{1,0:T(8,128)S(1)} %rev.87, f32[]{:T(128)} %bitcast.540, f32[]{:T(128)} %bitcast.541, f32[]{:T(128)} %bitcast.542, f32[]{:T(128)} %bitcast.543, f32[]{:T(128)} %bitcast.544, f32[]{:T(128)} %bitcast.545, f32[]{:T(128)} %bitcast.546, f32[]{:T(128)} %bitcast.547, f32[]{:T(128)} %bitcast.548, ...), kind=kLoop, calls=%fused_computation.195.clone.1 | loop fusion | flops 12451840 | bytes 526976 | tf_op jit(solution)/shard_map/while/body/eval_jaxpr/while/body/eval_jaxpr/jvp()/add | solution.py:37
  699.5 3.8 fusion.241
  705.1 3.6 fusion.242
  721.5 21.7 %add_add_fusion.8 = f32[512,128]{1,0:T(8,128)S(1)} fusion(f32[512,128]{1,0:T(8,128)S(1)} %rev.87, f32[]{:T(128)} %bitcast.540, f32[]{:T(128)} %bitcast.541, f32[]{:T(128)} %bitcast.542, f32[]{:T(128)} %bitcast.543, f32[]{:T(128)} %bitcast.544, f32[]{:T(128)} %bitcast.545, f32[]{:T(128)} %bitcast.546, f32[]{:T(128)} %bitcast.547, f32[]{:T(128)} %bitcast.548, ...), kind=kLoop, calls=%fused_computation.195.clone.1 | loop fusion | flops 12451840 | bytes 526976 | tf_op jit(solution)/shard_map/while/body/eval_jaxpr/while/body/eval_jaxpr/jvp()/add | solution.py:37
  743.6 3.8 fusion.241
  749.1 3.6 fusion.242
  752.7 2.6 bitcast_add_fusion.11
  756.6 7.0 reduce-scatter.2.cloned.1.call-done
  765.2 120.6 %all-reduce.37.cloned.1.call-done = f32[16,1024]{1,0:T(8,128)} async-done(((f32[16,1024]{1,0:T(8,128)}), f32[16,1024]{1,0:T(8,128)}) %all-reduce.37.cloned.1.call-update) | async-done | bytes 65552 | tf_op jit(solution)/shard_map/psum | solution.py:158
  (277 shorter events, 114.9 us)
Async XLA Ops:
  7.2 354.9 %copy-start = (bf16[1,128,1024]{2,1,0:T(8,128)(2,1)S(1)}, bf16[1,128,1024]{2,1,0:T(8,128)(2,1)}, u32[]{:S(2)}) copy-start(bf16[1,128,1024]{2,1,0:T(8,128)(2,1)} %param.20) | copy-start | bytes 786436
  7.2 94.6 %copy-start.6 = (bf16[1,128,1024]{2,1,0:T(8,128)(2,1)S(1)}, bf16[1,128,1024]{2,1,0:T(8,128)(2,1)}, u32[]{:S(2)}) copy-start(bf16[1,128,1024]{2,1,0:T(8,128)(2,1)} %param.16) | copy-start | bytes 786436
  7.2 6.5 copy-start.20
  7.2 6.9 copy-start.19
  7.2 94.6 %copy-start.18 = (f32[1024]{0:T(1024)S(1)}, f32[1024]{0:T(1024)}, u32[]{:S(2)}) copy-start(f32[1024]{0:T(1024)} %param.24) | copy-start | bytes 12292
  7.2 94.6 %copy-start.1 = (f32[32]{0:T(128)S(1)}, f32[32]{0:T(128)}, u32[]{:S(2)}) copy-start(f32[32]{0:T(128)} %param.25) | copy-start | bytes 388
  7.2 50.4 %all-gather.13.cloned.1.call-start = ((), (), s32[]{:S(2)}) async-start(), calls=%async_computation.5 | async-start | bytes 2359296 | tf_op jit(solution)/shard_map/all_gather | solution.py:107
  9.2 92.6 %all-gather.15.cloned.1.call-start = ((), (), s32[]{:S(2)}) async-start(), calls=%async_computation.6 | async-start | bytes 2359296 | tf_op jit(solution)/shard_map/all_gather | solution.py:106
  11.1 351.0 %all-gather.9.cloned.1.call-start = ((), (), s32[]{:S(2)}) async-start(), calls=%async_computation.1 | async-start | bytes 2129920 | tf_op jit(solution)/shard_map/all_gather | solution.py:145
  11.8 655.2 %all-gather.17.cloned.1.call-start = ((), (), s32[]{:S(2)}) async-start(), calls=%async_computation.7 | async-start | bytes 2359296 | tf_op jit(solution)/shard_map/all_gather | solution.py:219
  13.7 653.3 %all-gather.11.cloned.1.call-start = ((), (), s32[]{:S(2)}) async-start(), calls=%async_computation.2 | async-start | bytes 2359296 | tf_op jit(solution)/shard_map/all_gather | solution.py:220
  133.2 3.1 copy-start.9
  169.6 3.1 copy-start.9
  175.9 189.9 %copy-start.13 = (bf16[128,1024]{1,0:T(8,128)(2,1)}, bf16[128,1024]{1,0:T(8,128)(2,1)S(1)}, u32[]{:S(2)}) copy-start(bf16[128,1024]{1,0:T(8,128)(2,1)S(1)} %copy.114) | copy-start | bytes 786436
  175.9 188.7 %copy-start.16 = (bf16[1,128,1024]{2,1,0:T(8,128)(2,1)S(1)}, bf16[1,128,1024]{2,1,0:T(8,128)(2,1)}, u32[]{:S(2)}) copy-start(bf16[1,128,1024]{2,1,0:T(8,128)(2,1)} %param.19) | copy-start | bytes 786436
  365.7 397.9 %reduce-scatter.2.cloned.1.call-start = ((), (), s32[]{:S(2)}) async-start(), calls=%async_computation.3 | async-start | bytes 4259840 | tf_op jit(solution)/shard_map/reduce_scatter | solution.py:150
  368.6 517.2 %all-reduce.37.cloned.1.call-start = ((), (), s32[]{:S(2)}) async-start(), calls=%async_computation.4 | async-start | bytes 131072 | tf_op jit(solution)/shard_map/psum | solution.py:158
  410.9 2.0 copy-start.17
  418.1 4.6 copy-start.8
  486.2 2.0 copy-start.17
  493.5 4.6 copy-start.8
  668.2 2.8 copy-start.12
  671.1 3.0 copy-start.2
  699.2 4.1 copy-start.15
  699.5 5.5 copy-start.3
  699.5 5.5 copy-start.5
  712.2 2.8 copy-start.12
  715.1 3.0 copy-start.2
  743.2 4.1 copy-start.15
  743.6 5.5 copy-start.3
  743.6 5.5 copy-start.5
  755.3 9.1 %copy-start.11 = (f32[128,1024]{0,1:T(8,128)S(1)}, f32[128,1024]{0,1:T(8,128)}, u32[]{:S(2)}) copy-start(f32[128,1024]{0,1:T(8,128)} %get-tuple-element.955) | copy-start | bytes 1572868
  (7 other events, 9.0 us)
Sparse Core Ops, SparseCore 0:
  10.8 46.8 all-gather.12
  60.4 41.4 all-gather.14
  103.9 258.0 all-gather.8
  364.0 82.6 all-gather.16
  449.3 37.8 all-gather.10
  489.8 273.7 reduce-scatter.1
  766.8 119.0 all-reduce.36
where the time goes:
time: 899 us; the launch traced here: 894 us
  waiting for transfers between devices  402 us (45%)
  other arithmetic  193 us (21%)
  blocking collectives  141 us (16%)
  local copies, waits for them, and re-layouts  97.3 us (11%)
  matrix products  40.8 us (5%)
  between operations  14.3 us (2%)
    all_gather x1, waiting for transfers between devices, on_device(): whole_rows = lax.all_gather(out_weight, 'dp', axis=0, tiled=True)  186 us
    psum x1, blocking collectives, on_device(): pos_grad, time_grad = lax.psum((pos_local, time_local), ('dp', 'ctx'))  141 us
    add x6, other arithmetic, block_bias(): return toeplitz(pos_table, offset, row_total, col_total) + timed  132 us
    psum x1, waiting for transfers between devices, on_device(): weight_grad = lax.psum(weight_part, 'ctx')  121 us
    all_gather x1, waiting for transfers between devices, on_device(): lax.all_gather(key_mine, 'ctx', axis=0, tiled=True)  44.1 us
    all_gather x1, waiting for transfers between devices, on_device(): lax.all_gather(value_mine, 'ctx', axis=0, tiled=True)  43.6 us
    add x2, other arithmetic, query_per_key(): carried[2] + time_part  40.2 us
  transfers between devices with their start and end apart: 7, of which 5 were waited for; matrix products, arithmetic and copies ran while one was open for 36% of the time, Pallas kernels for 0%

commit v1 on v0

--- a/solution.py
+++ b/solution.py
@@ -155,7 +155,7 @@
         scatter_dimension=0,
         tiled=True,
     )
-    weight_grad = lax.psum(weight_part, "ctx")
+    weight_grad = jnp.sum(lax.all_gather(weight_part, "ctx"), axis=0)
     gate_grad = (mixed_grad * normed).astype(jnp.bfloat16)
     normed_grad = mixed_grad * gate_wide
     attn_grad = inv_dev * (

time: 899 us -> 843 us (0.938)
  the two profiles are of different devices: /device:TPU:17 before, /device:TPU:1 now
where the time goes in v1:
time: 843 us; the launch traced here: 839 us
  waiting for transfers between devices  285 us (34%)
  blocking collectives  207 us (25%)
  other arithmetic  194 us (23%)
  local copies, waits for them, and re-layouts  92.8 us (11%)
  matrix products  40.7 us (5%)
  between operations  14.3 us (2%)
    all_gather x1, waiting for transfers between devices, on_device(): whole_rows = lax.all_gather(out_weight, 'dp', axis=0, tiled=True)  189 us
    psum x1, blocking collectives, on_device(): pos_grad, time_grad = lax.psum((pos_local, time_local), ('dp', 'ctx'))  142 us
    add x6, other arithmetic, block_bias(): return toeplitz(pos_table, offset, row_total, col_total) + timed  132 us
    all_gather x1, blocking collectives, on_device(): weight_grad = jnp.sum(lax.all_gather(weight_part, 'ctx'), axis=0)  65.4 us
    all_gather x1, waiting for transfers between devices, on_device(): lax.all_gather(value_mine, 'ctx', axis=0, tiled=True)  45.8 us
    all_gather x1, waiting for transfers between devices, on_device(): lax.all_gather(key_mine, 'ctx', axis=0, tiled=True)  44.1 us
    add x2, other arithmetic, query_per_key(): carried[2] + time_part  40.2 us
    while x70, local copies, waits for them, and re-layouts  18.9 us
  transfers between devices with their start and end apart: 6, of which 4 were waited for; matrix products, arithmetic and copies ran while one was open for 38% of the time, Pallas kernels for 0%

profile of v1, /device:TPU:1, one launch (start us, length us, event | category | flops | bytes accessed | tf_op | source)
XLA Modules:
  0.0 838.9 jit_solution(15680357455193889982)
XLA Ops:
  14.0 45.8 %all-gather.14.cloned.1.call-done = bf16[1,1024,1024]{1,2,0:T(8,128)(2,1)} async-done(((bf16[1,128,1024]{1,2,0:T(8,128)(2,1)}), bf16[1,1024,1024]{1,2,0:T(8,128)(2,1)}) %all-gather.14.cloned.1.call-update) | async-done | bytes 2097168 | tf_op jit(solution)/shard_map/all_gather | solution.py:107
  59.8 44.1 %all-gather.16.cloned.1.call-done = bf16[1,1024,1024]{1,2,0:T(8,128)(2,1)} async-done(((bf16[1,128,1024]{1,2,0:T(8,128)(2,1)}), bf16[1,1024,1024]{1,2,0:T(8,128)(2,1)}) %all-gather.16.cloned.1.call-update) | async-done | bytes 2097168 | tf_op jit(solution)/shard_map/all_gather | solution.py:106
  104.0 68.7 %while.78 = (s32[]{:T(128)}, f32[128,1024]{0,1:T(8,128)}, s32[2]{0:T(128)S(1)}, bf16[1024,1024]{0,1:T(8,128)(2,1)}, s32[128]{0:T(128)S(1)}, /*index=5*/s32[1024]...) while((s32[]{:T(128)}, f32[128,1024]{0,1:T(8,128)}, ...), condition=%wide.region_3.4_spmd.clone, body=%wide.region_2.3_spmd.clone.sunk | while | flops 285542272 | bytes 18211576 | solution.py:131
  109.4 21.8 %add_add_fusion.6 = f32[128,512]{1,0:T(8,128)S(1)} fusion(f32[128,512]{1,0:T(8,128)S(1)} %rev.84, f32[]{:T(128)} %bitcast.418, f32[]{:T(128)} %bitcast.419, f32[]{:T(128)} %bitcast.420, f32[]{:T(128)} %bitcast.421, f32[]{:T(128)} %bitcast.422, f32[]{:T(128)} %bitcast.423, f32[]{:T(128)} %bitcast.424, f32[]{:T(128)} %bitcast.425, f32[]{:T(128)} %bitcast.426, ...), kind=kLoop, calls=%fused_computation.10.clone.1 | loop fusion | flops 12451840 | bytes 526976 | tf_op jit(solution)/shard_map/while/body/eval_jaxpr/while/body/eval_jaxpr/jvp()/add | solution.py:37
  133.3 3.0 fusion.217
  143.7 21.8 %add_add_fusion.6 = f32[128,512]{1,0:T(8,128)S(1)} fusion(f32[128,512]{1,0:T(8,128)S(1)} %rev.84, f32[]{:T(128)} %bitcast.418, f32[]{:T(128)} %bitcast.419, f32[]{:T(128)} %bitcast.420, f32[]{:T(128)} %bitcast.421, f32[]{:T(128)} %bitcast.422, f32[]{:T(128)} %bitcast.423, f32[]{:T(128)} %bitcast.424, f32[]{:T(128)} %bitcast.425, f32[]{:T(128)} %bitcast.426, ...), kind=kLoop, calls=%fused_computation.10.clone.1 | loop fusion | flops 12451840 | bytes 526976 | tf_op jit(solution)/shard_map/while/body/eval_jaxpr/while/body/eval_jaxpr/jvp()/add | solution.py:37
  167.6 3.0 fusion.217
  174.2 188.8 %all-gather.10.cloned.1.call-done = bf16[1024,1024]{1,0:T(8,128)(2,1)} async-done(((bf16[16,1024]{1,0:T(8,128)(2,1)}), bf16[1024,1024]{1,0:T(8,128)(2,1)}) %all-gather.10.cloned.1.call-update) | async-done | bytes 2097168 | tf_op jit(solution)/shard_map/all_gather | solution.py:145
  363.0 2.5 fusion.156
  367.0 2.8 fusion.152
  371.3 150.5 %while.79 = (s32[]{:T(128)}, f32[128,1024]{0,1:T(8,128)}, f32[1024]{0:T(1024)S(1)}, f32[32]{0:T(128)S(1)}, s32[2]{0:T(128)S(1)}, /*index=5*/bf16[1024,1024]{0,1:...) while((s32[]{:T(128)}, f32[128,1024]{0,1:T(8,128)}, ...), condition=%wide.region_43.44_spmd.clone, body=%wide.region_8.43_spmd.clone.sunk | while | flops 434852608 | bytes 32417576 | solution.py:204
  385.0 3.1 rev.85
  389.6 22.5 %add_add_fusion.7 = f32[128,512]{0,1:T(8,128)S(1)} fusion(f32[128,512]{0,1:T(8,128)} %rev.85, f32[]{:T(128)} %bitcast.462, f32[]{:T(128)} %bitcast.463, f32[]{:T(128)} %bitcast.464, f32[]{:T(128)} %bitcast.465, f32[]{:T(128)} %bitcast.466, f32[]{:T(128)} %bitcast.467, f32[]{:T(128)} %bitcast.468, f32[]{:T(128)} %bitcast.469, f32[]{:T(128)} %bitcast.470, ...), kind=kLoop, calls=%fused_computation.100.clone.1 | loop fusion | flops 12451840 | bytes 526976 | tf_op jit(solution)/shard_map/while/body/eval_jaxpr/while/body/eval_jaxpr/jvp()/add | solution.py:37
  423.9 2.5 select_reduce_fusion.33
  426.4 20.1 %fusion.230 = f32[32]{0:T(128)S(1)} fusion(f32[32]{0:T(128)S(1)} %get-tuple-element.2032, pred[]{:T(512)S(6)} %compare.44, f32[1]{0:T(128)} %bitcast.498, f32[1]{0:T(128)} %bitcast.499, f32[1]{0:T(128)} %bitcast.500, f32[1]{0:T(128)} %bitcast.501, f32[1]{0:T(128)} %bitcast.502, f32[1]{0:T(128)} %bitcast.503, f32[1]{0:T(128)} %bitcast.504, ...), kind=kLoop, calls=%fused_computation.175.clone.1 | loop fusion | flops 1056 | bytes 385 | tf_op jit(solution)/shard_map/while/body/eval_jaxpr/while/body/eval_jaxpr/add | solution.py:194
  447.7 2.5 constant_dynamic-slice_fusion.11
  460.2 3.1 rev.85
  464.8 22.5 %add_add_fusion.7 = f32[128,512]{0,1:T(8,128)S(1)} fusion(f32[128,512]{0,1:T(8,128)} %rev.85, f32[]{:T(128)} %bitcast.462, f32[]{:T(128)} %bitcast.463, f32[]{:T(128)} %bitcast.464, f32[]{:T(128)} %bitcast.465, f32[]{:T(128)} %bitcast.466, f32[]{:T(128)} %bitcast.467, f32[]{:T(128)} %bitcast.468, f32[]{:T(128)} %bitcast.469, f32[]{:T(128)} %bitcast.470, ...), kind=kLoop, calls=%fused_computation.100.clone.1 | loop fusion | flops 12451840 | bytes 526976 | tf_op jit(solution)/shard_map/while/body/eval_jaxpr/while/body/eval_jaxpr/jvp()/add | solution.py:37
  499.2 2.5 select_reduce_fusion.33
  501.8 20.1 %fusion.230 = f32[32]{0:T(128)S(1)} fusion(f32[32]{0:T(128)S(1)} %get-tuple-element.2032, pred[]{:T(512)S(6)} %compare.44, f32[1]{0:T(128)} %bitcast.498, f32[1]{0:T(128)} %bitcast.499, f32[1]{0:T(128)} %bitcast.500, f32[1]{0:T(128)} %bitcast.501, f32[1]{0:T(128)} %bitcast.502, f32[1]{0:T(128)} %bitcast.503, f32[1]{0:T(128)} %bitcast.504, ...), kind=kLoop, calls=%fused_computation.175.clone.1 | loop fusion | flops 1056 | bytes 385 | tf_op jit(solution)/shard_map/while/body/eval_jaxpr/while/body/eval_jaxpr/add | solution.py:194
  523.1 141.6 %all-reduce.34 = (f32[1024]{0:T(1024)}, f32[32]{0:T(128)}) all-reduce(f32[1024]{0:T(1024)S(1)} %get-tuple-element.956, f32[32]{0:T(128)S(1)} %get-tuple-element.957), channel_id=1, replica_groups=mesh['dp'=64,'ctx'=8] {'dp','ctx'}, use_global_device_ids=true, to_apply=%region_48.49 | all-reduce | flops 1056 | bytes 8448 | tf_op jit(solution)/shard_map/psum | solution.py:270
  664.7 3.0 fusion.136
  668.5 88.4 %while.80 = (s32[]{:T(128)}, f32[128,1024]{0,1:T(8,128)}, f32[128,1024]{0,1:T(8,128)}, s32[2]{0:T(128)S(1)}, bf16[1024,1024]{0,1:T(8,128)(2,1)}, /*index=5*/s32[...) while((s32[]{:T(128)}, f32[128,1024]{0,1:T(8,128)}, ...), condition=%wide.region_45.46_spmd.clone, body=%wide.region_44.45_spmd.clone.sunk | while | flops 560531328 | bytes 61329784 | solution.py:258
  679.0 21.7 %add_add_fusion.8 = f32[512,128]{1,0:T(8,128)S(1)} fusion(f32[512,128]{1,0:T(8,128)S(1)} %rev.87, f32[]{:T(128)} %bitcast.541, f32[]{:T(128)} %bitcast.542, f32[]{:T(128)} %bitcast.543, f32[]{:T(128)} %bitcast.544, f32[]{:T(128)} %bitcast.545, f32[]{:T(128)} %bitcast.546, f32[]{:T(128)} %bitcast.547, f32[]{:T(128)} %bitcast.548, f32[]{:T(128)} %bitcast.549, ...), kind=kLoop, calls=%fused_computation.195.clone.1 | loop fusion | flops 12451840 | bytes 526976 | tf_op jit(solution)/shard_map/while/body/eval_jaxpr/while/body/eval_jaxpr/jvp()/add | solution.py:37
  701.0 3.8 fusion.241
  706.6 3.6 fusion.242
  723.0 21.7 %add_add_fusion.8 = f32[512,128]{1,0:T(8,128)S(1)} fusion(f32[512,128]{1,0:T(8,128)S(1)} %rev.87, f32[]{:T(128)} %bitcast.541, f32[]{:T(128)} %bitcast.542, f32[]{:T(128)} %bitcast.543, f32[]{:T(128)} %bitcast.544, f32[]{:T(128)} %bitcast.545, f32[]{:T(128)} %bitcast.546, f32[]{:T(128)} %bitcast.547, f32[]{:T(128)} %bitcast.548, f32[]{:T(128)} %bitcast.549, ...), kind=kLoop, calls=%fused_computation.195.clone.1 | loop fusion | flops 12451840 | bytes 526976 | tf_op jit(solution)/shard_map/while/body/eval_jaxpr/while/body/eval_jaxpr/jvp()/add | solution.py:37
  745.1 3.8 fusion.241
  750.6 3.6 fusion.242
  754.2 2.6 bitcast_add_fusion.11
  760.7 5.2 reduce-scatter.2.cloned.1.call-done
  766.0 65.4 %all-gather.3 = f32[128,1024]{1,0:T(8,128)S(1)} all-gather(f32[16,1024]{1,0:T(8,128)} %reduce-scatter.2.cloned.1.call-done), channel_id=5, replica_groups=mesh['dp'=64,'ctx'=8] {'ctx'}, dimensions={0}, use_global_device_ids=true | all-gather | bytes 589824 | tf_op jit(solution)/shard_map/all_gather | solution.py:158
  (271 shorter events, 111.1 us)
Async XLA Ops:
  7.2 355.9 %copy-start = (bf16[1,128,1024]{2,1,0:T(8,128)(2,1)S(1)}, bf16[1,128,1024]{2,1,0:T(8,128)(2,1)}, u32[]{:S(2)}) copy-start(bf16[1,128,1024]{2,1,0:T(8,128)(2,1)} %param.20) | copy-start | bytes 786436
  7.2 6.5 copy-start.18
  7.2 6.8 copy-start.17
  7.2 96.8 %copy-start.16 = (f32[1024]{0:T(1024)S(1)}, f32[1024]{0:T(1024)}, u32[]{:S(2)}) copy-start(f32[1024]{0:T(1024)} %param.24) | copy-start | bytes 12292
  7.2 96.8 %copy-start.1 = (f32[32]{0:T(128)S(1)}, f32[32]{0:T(128)}, u32[]{:S(2)}) copy-start(f32[32]{0:T(128)} %param.25) | copy-start | bytes 388
  7.2 52.6 %all-gather.14.cloned.1.call-start = ((), (), s32[]{:S(2)}) async-start(), calls=%async_computation.4 | async-start | bytes 2359296 | tf_op jit(solution)/shard_map/all_gather | solution.py:107
  9.1 94.9 %all-gather.16.cloned.1.call-start = ((), (), s32[]{:S(2)}) async-start(), calls=%async_computation.5 | async-start | bytes 2359296 | tf_op jit(solution)/shard_map/all_gather | solution.py:106
  11.0 352.0 %all-gather.10.cloned.1.call-start = ((), (), s32[]{:S(2)}) async-start(), calls=%async_computation.1 | async-start | bytes 2129920 | tf_op jit(solution)/shard_map/all_gather | solution.py:145
  11.7 656.7 %all-gather.18.cloned.1.call-start = ((), (), s32[]{:S(2)}) async-start(), calls=%async_computation.6 | async-start | bytes 2359296 | tf_op jit(solution)/shard_map/all_gather | solution.py:219
  13.6 654.9 %all-gather.12.cloned.1.call-start = ((), (), s32[]{:S(2)}) async-start(), calls=%async_computation.2 | async-start | bytes 2359296 | tf_op jit(solution)/shard_map/all_gather | solution.py:220
  133.3 3.0 copy-start.8
  167.6 3.0 copy-start.8
  173.8 193.1 %copy-start.11 = (bf16[128,1024]{1,0:T(8,128)(2,1)}, bf16[128,1024]{1,0:T(8,128)(2,1)S(1)}, u32[]{:S(2)}) copy-start(bf16[128,1024]{1,0:T(8,128)(2,1)S(1)} %copy.114) | copy-start | bytes 786436
  173.9 191.7 %copy-start.14 = (bf16[1,128,1024]{2,1,0:T(8,128)(2,1)S(1)}, bf16[1,128,1024]{2,1,0:T(8,128)(2,1)}, u32[]{:S(2)}) copy-start(bf16[1,128,1024]{2,1,0:T(8,128)(2,1)} %param.19) | copy-start | bytes 786436
  366.7 399.3 %reduce-scatter.2.cloned.1.call-start = ((), (), s32[]{:S(2)}) async-start(), calls=%async_computation.3 | async-start | bytes 4259840 | tf_op jit(solution)/shard_map/reduce_scatter | solution.py:150
  369.7 1.6 copy-start.4
  412.1 2.0 copy-start.6
  412.1 2.0 copy-start.15
  419.3 4.6 copy-start.7
  487.3 1.9 copy-start.6
  487.3 2.0 copy-start.15
  494.6 4.6 copy-start.7
  669.7 2.8 copy-start.10
  672.6 3.0 copy-start.2
  700.7 4.1 copy-start.13
  701.0 5.5 copy-start.3
  701.0 5.5 copy-start.5
  713.7 2.8 copy-start.10
  716.7 3.0 copy-start.2
  744.7 4.1 copy-start.13
  745.1 5.5 copy-start.3
  745.1 5.5 copy-start.5
  (4 other events, 3.5 us)
Sparse Core Ops, SparseCore 0:
  10.7 49.0 all-gather.13
  62.5 41.4 all-gather.15
  106.1 256.8 all-gather.9
  365.0 83.7 all-gather.17
  451.4 37.0 all-gather.11
  491.1 274.8 reduce-scatter.1
